TPU v7x, 256 devices: a whole 4x4x8 slice. The times are simulated.
256 devices in a mesh: row: 64 (over z_hi, y, x, core), col: 4 (over z_lo).
Axes of the slice: x: 4, y: 4, z: 8 (z_hi: 2, z_lo: 4; z = z_hi * 4 + z_lo), core: 2. Of those that a mesh axis runs over, the one named last changes fastest.
Arguments:
- block_rows: int32 [64, 4, 64], P('row', 'col'), may hold values from -1 to 251, as said below
- block_cols: int32 [64, 4, 64], P('row', 'col'), may hold values from -1 to 255, as said below
- block_values: bfloat16 [64, 4, 64, 256, 256], P('row', 'col'), may hold values from 0.0009994507 to 1
- near_values: bfloat16 [65536, 1024], P(('row', 'col')), may hold values from 0.0009994507 to 1
- hole_ids: int32 [65536], P(('row', 'col')), may hold values from 0 to 199
- start_codes: float32 [200, 64], replicated, may hold values from -6 to 6
Outputs:
- basis: float32 [65536, 64], P(('row', 'col'))
Inputs may be any that keep to these rules, and one draw needn't show every extreme that they name: `block_rows`: A live slot of the device at band r and column index c names a block row of band r and a block column j * 4 + c * 4 / 4 + i with j > r and 0 <= i < 4 / 4. The device at band r has exactly (64 * (64 - 1 - r) + 64 - 2) // (64 - 1) live slots, placed first; the others hold -1 in both lists and their values are ignored. A block may be named by several slots; the affinity is then the sum. `block_cols`: see block_rows; empty slots hold -1 in the same places.
All inputs are finite; a program needn't handle non-finite values.
Results may differ from a plain program's by a relative error of at most 0.0063.
Values may be sent and summed in bfloat16 or wider, within the bound.
A program may use at most 128 MiB of HBM per device.

v0:
```python
import jax
import jax.numpy as jnp
from jax import lax
from jax.sharding import PartitionSpec as P

ITERS = 3


def shards(block_rows, block_cols, block_values, near_values, hole_ids, start_codes):
    row_index = lax.axis_index("row")
    col_index = lax.axis_index("col")
    row_devices = lax.axis_size("row")
    col_devices = lax.axis_size("col")
    slot_count = block_rows.shape[2]
    block_size = block_values.shape[3]
    own_rows = near_values.shape[0]
    band_rows = near_values.shape[1]
    band_blocks = band_rows // block_size
    quarter_blocks = band_blocks // col_devices
    set_blocks = row_devices * quarter_blocks
    slot_rows = block_rows.reshape(slot_count)
    slot_cols = block_cols.reshape(slot_count)
    slot_vals = block_values.reshape(slot_count, block_size, block_size)
    live_slot = slot_rows >= 0
    local_row = jnp.where(live_slot, slot_rows - row_index * band_blocks, 0)
    local_col = jnp.where(
        live_slot,
        slot_cols // band_blocks * quarter_blocks
        + slot_cols % band_blocks
        - col_index * quarter_blocks,
        0,
    )
    weight_live = live_slot.astype(jnp.float32)
    pick_rows = (
        (local_row[:, None] == jnp.arange(band_blocks)[None, :]) & live_slot[:, None]
    ).astype(jnp.float32)
    own_first = row_index * own_rows

    def products(set_probe, band_probe, own_probe):
        col_width = set_probe.shape[1]
        set_tiles = set_probe.reshape(set_blocks, block_size, col_width)
        band_tiles = band_probe.reshape(band_blocks, block_size, col_width)
        forward = jnp.einsum(
            "sij,sjk->sik", slot_vals, set_tiles[local_col], preferred_element_type=jnp.float32
        )
        band_part = jnp.einsum(
            "sb,sik->bik", pick_rows, forward, precision=lax.Precision.HIGHEST
        ).reshape(band_rows, col_width)
        band_part = band_part + jnp.einsum(
            "ij,ik->jk", near_values, own_probe, preferred_element_type=jnp.float32
        )
        backward = (
            jnp.einsum(
                "sji,sjk->sik", slot_vals, band_tiles[local_row], preferred_element_type=jnp.float32
            )
            * weight_live[:, None, None]
        )
        own_sum = lax.psum_scatter(band_part, "col", scatter_dimension=0, tiled=True) + jnp.dot(
            near_values, band_probe, preferred_element_type=jnp.float32
        )
        set_part = jax.ops.segment_sum(backward, local_col, num_segments=set_blocks).reshape(
            set_blocks * block_size, col_width
        )
        current = lax.dynamic_slice_in_dim(set_part, own_first, own_rows, 0)
        set_part = lax.dynamic_update_slice_in_dim(set_part, current + own_sum, own_first, 0)
        return lax.psum_scatter(set_part, "row", scatter_dimension=0, tiled=True)

    set_total = set_blocks * block_size
    degree = products(
        jnp.ones((set_total, 1), jnp.bfloat16),
        jnp.ones((band_rows, 1), jnp.bfloat16),
        jnp.ones((own_rows, 1), jnp.bfloat16),
    )[:, 0]
    scale_root = 1.0 / jnp.sqrt(degree)
    onehot = (hole_ids[:, None] == jnp.arange(start_codes.shape[0])[None, :]).astype(jnp.float32)
    basis_now = jnp.dot(onehot, start_codes, precision=lax.Precision.HIGHEST)
    total_rows = own_rows * row_devices * col_devices
    for sweep_index in range(ITERS):
        own_probe = (scale_root[:, None] * basis_now).astype(jnp.bfloat16)
        set_probe = lax.all_gather(own_probe, "row", axis=0, tiled=True)
        band_probe = lax.all_gather(own_probe, "col", axis=0, tiled=True)
        image = scale_root[:, None] * products(set_probe, band_probe, own_probe)
        local_gram = jnp.dot(image.T, image, precision=lax.Precision.HIGHEST)
        gram_matrix = lax.psum(local_gram, ("row", "col")) / total_rows
        factor = jnp.linalg.cholesky(gram_matrix)
        basis_now = lax.linalg.triangular_solve(
            factor, image, left_side=False, lower=True, transpose_a=True
        )
    return basis_now


def solution(mesh):
    return jax.shard_map(
        shards,
        mesh=mesh,
        in_specs=(
            P("row", "col", None),
            P("row", "col", None),
            P("row", "col", None, None, None),
            P(("row", "col"), None),
            P(("row", "col")),
            P(),
        ),
        out_specs=P(("row", "col"), None),
        check_vma=False,
    )
```

profile of v0, /device:TPU:1, one launch (start us, length us, event | category | flops | bytes accessed | tf_op | source)
XLA Modules:
  0.0 2392.6 jit_solution(8362141626464037936)
XLA Ops:
  9.3 5.6 fusion.12
  22.8 22.8 reduce-scatter.25.cloned.1.call-done
  46.8 4.9 copy.58
  51.8 417.7 %reduce-scatter.27.cloned.1.call-done = f32[256,1]{1,0:T(8,128)} async-done(((f32[16384,1]{1,0:T(8,128)}), f32[256,1]{1,0:T(8,128)}) %reduce-scatter.27.cloned.1.call-update) | async-done | bytes 1040
  471.6 11.5 all_gather.18
  483.8 78.4 %all-gather.4.cloned.1.call-done = bf16[16384,64]{0,1:T(8,128)(2,1)} async-done(((bf16[256,64]{0,1:T(8,128)(2,1)}), bf16[16384,64]{0,1:T(8,128)(2,1)}) %all-gather.4.cloned.1.call-update) | async-done | bytes 2097168 | tf_op jit(solution)/shard_map/all_gather | solution.py:80
  569.0 6.6 fusion.22
  580.4 12.4 reduce-scatter.15.cloned.1.call-start
  592.8 6.9 multiply_bitcast_fusion.2
  602.2 13.6 scatter_fusion
  622.1 404.8 %reduce-scatter.15.cloned.1.call-done = f32[256,64]{0,1:T(8,128)} async-done(((f32[16384,64]{0,1:T(8,128)}), f32[256,64]{0,1:T(8,128)}) %reduce-scatter.15.cloned.1.call-update) | async-done | bytes 65552 | tf_op jit(solution)/shard_map/reduce_scatter | solution.py:66
  1028.1 81.2 %psum.21 = f32[64,64]{0,1:T(8,128)S(1)} all-reduce(f32[64,64]{0,1:T(8,128)S(1)} %fusion.71), channel_id=1, replica_groups=mesh['row'=64,'col'=4] {'row','col'}, use_global_device_ids=true, to_apply=%region_6.7 | all-reduce | flops 4096 | bytes 32768 | tf_op jit(solution)/shard_map/psum | solution.py:84
  1109.4 5.8 cholesky.59
  1116.5 4.9 custom-call.7
  1123.2 10.7 all_gather.20
  1134.6 71.2 %all-gather.6.cloned.1.call-done = bf16[16384,64]{0,1:T(8,128)(2,1)} async-done(((bf16[256,64]{0,1:T(8,128)(2,1)}), bf16[16384,64]{0,1:T(8,128)(2,1)}) %all-gather.6.cloned.1.call-update) | async-done | bytes 2097168 | tf_op jit(solution)/shard_map/all_gather | solution.py:80
  1212.6 6.6 fusion.25
  1224.1 6.9 multiply_bitcast_fusion.1
  1233.5 13.6 scatter_fusion.1
  1253.4 404.8 %reduce-scatter.19.cloned.1.call-done = f32[256,64]{0,1:T(8,128)} async-done(((f32[16384,64]{0,1:T(8,128)}), f32[256,64]{0,1:T(8,128)}) %reduce-scatter.19.cloned.1.call-update) | async-done | bytes 65552 | tf_op jit(solution)/shard_map/reduce_scatter | solution.py:66
  1659.4 81.3 %psum.22 = f32[64,64]{0,1:T(8,128)S(1)} all-reduce(f32[64,64]{0,1:T(8,128)S(1)} %fusion.68), channel_id=1, replica_groups=mesh['row'=64,'col'=4] {'row','col'}, use_global_device_ids=true, to_apply=%region_12.15 | all-reduce | flops 4096 | bytes 32768 | tf_op jit(solution)/shard_map/psum | solution.py:84
  1740.7 5.8 cholesky.70
  1747.9 4.9 custom-call.8
  1754.8 10.7 all_gather.22
  1766.2 70.8 %all-gather.8.cloned.1.call-done = bf16[16384,64]{0,1:T(8,128)(2,1)} async-done(((bf16[256,64]{0,1:T(8,128)(2,1)}), bf16[16384,64]{0,1:T(8,128)(2,1)}) %all-gather.8.cloned.1.call-update) | async-done | bytes 2097168 | tf_op jit(solution)/shard_map/all_gather | solution.py:80
  1843.7 6.6 fusion.28
  1855.2 6.9 multiply_bitcast_fusion
  1864.6 13.6 scatter_fusion.2
  1884.5 404.6 %reduce-scatter.23.cloned.1.call-done = f32[256,64]{0,1:T(8,128)} async-done(((f32[16384,64]{0,1:T(8,128)}), f32[256,64]{0,1:T(8,128)}) %reduce-scatter.23.cloned.1.call-update) | async-done | bytes 65552 | tf_op jit(solution)/shard_map/reduce_scatter | solution.py:66
  2290.3 81.6 %psum.23 = f32[64,64]{0,1:T(8,128)S(1)} all-reduce(f32[64,64]{0,1:T(8,128)S(1)} %fusion.65), channel_id=1, replica_groups=mesh['row'=64,'col'=4] {'row','col'}, use_global_device_ids=true, to_apply=%region_16.19 | all-reduce | flops 4096 | bytes 32768 | tf_op jit(solution)/shard_map/psum | solution.py:84
  2371.9 5.8 cholesky.81
  2379.1 4.9 custom-call.9
  (112 shorter events, 90.4 us)
Async XLA Ops:
  6.5 8.6 copy-start
  6.5 39.1 %reduce-scatter.25.cloned.1.call-start = ((), (), s32[]{:S(2)}) async-start(), calls=%async_computation.17 | async-start | bytes 655360
  16.4 453.1 %reduce-scatter.27.cloned.1.call-start = ((), (), s32[]{:S(2)}) async-start(), calls=%async_computation.18 | async-start | bytes 8519680
  51.7 418.8 %copy-start.4 = (f32[200,64]{0,1:T(8,128)S(1)}, f32[200,64]{0,1:T(8,128)}, u32[]{:S(2)}) copy-start(f32[200,64]{0,1:T(8,128)} %param.14) | copy-start | bytes 153604
  51.7 418.8 %copy-start.5 = (s32[256]{0:T(256)S(1)}, s32[256]{0:T(256)}, u32[]{:S(2)}) copy-start(s32[256]{0:T(256)} %param.13) | copy-start | bytes 3076
  51.8 510.4 %all-gather.4.cloned.1.call-start = ((), (), s32[]{:S(2)}) async-start(), calls=%async_computation.8 | async-start | bytes 2129920 | tf_op jit(solution)/shard_map/all_gather | solution.py:80
  471.5 148.7 %reduce-scatter.13.cloned.1.call-start = ((), (), s32[]{:S(2)}) async-start(), calls=%async_computation.9 | async-start | bytes 327680 | tf_op jit(solution)/shard_map/reduce_scatter | solution.py:58
  575.6 3.9 copy-start.3
  580.4 446.5 %reduce-scatter.15.cloned.1.call-start = ((), (), s32[]{:S(2)}) async-start(), calls=%async_computation.10 | async-start | bytes 4259840 | tf_op jit(solution)/shard_map/reduce_scatter | solution.py:66
  622.1 583.8 %all-gather.6.cloned.1.call-start = ((), (), s32[]{:S(2)}) async-start(), calls=%async_computation.11 | async-start | bytes 2129920 | tf_op jit(solution)/shard_map/all_gather | solution.py:80
  1123.2 128.4 %reduce-scatter.17.cloned.1.call-start = ((), (), s32[]{:S(2)}) async-start(), calls=%async_computation.12 | async-start | bytes 327680 | tf_op jit(solution)/shard_map/reduce_scatter | solution.py:58
  1219.3 3.9 copy-start.2
  1224.1 434.2 %reduce-scatter.19.cloned.1.call-start = ((), (), s32[]{:S(2)}) async-start(), calls=%async_computation.13 | async-start | bytes 4259840 | tf_op jit(solution)/shard_map/reduce_scatter | solution.py:66
  1253.4 583.6 %all-gather.8.cloned.1.call-start = ((), (), s32[]{:S(2)}) async-start(), calls=%async_computation.14 | async-start | bytes 2129920 | tf_op jit(solution)/shard_map/all_gather | solution.py:80
  1754.6 128.1 %reduce-scatter.21.cloned.1.call-start = ((), (), s32[]{:S(2)}) async-start(), calls=%async_computation.15 | async-start | bytes 327680 | tf_op jit(solution)/shard_map/reduce_scatter | solution.py:58
  1850.4 3.9 copy-start.1
  1855.2 433.9 %reduce-scatter.23.cloned.1.call-start = ((), (), s32[]{:S(2)}) async-start(), calls=%async_computation.16 | async-start | bytes 4259840 | tf_op jit(solution)/shard_map/reduce_scatter | solution.py:66
Sparse Core Ops, SparseCore 0:
  16.5 29.0 reduce-scatter.24
  51.9 417.5 reduce-scatter.26
  472.9 89.2 all-gather.3
  580.5 16.6 reduce-scatter.12
  622.2 404.7 reduce-scatter.14
  1123.3 82.4 all-gather.5
  1224.2 16.6 reduce-scatter.16
  1253.5 404.7 reduce-scatter.18
  1754.7 82.2 all-gather.7
  1855.3 16.6 reduce-scatter.20
  1884.6 404.4 reduce-scatter.22
where the time goes:
time: 2400 us; the launch traced here: 2390 us
  waiting for transfers between devices  1880 us (78%)
  blocking collectives  277 us (12%)
  matrix products  80.3 us (3%)
  other arithmetic  80.1 us (3%)
  local copies, waits for them, and re-layouts  53.2 us (2%)
    reduce_scatter x3, waiting for transfers between devices, products(): return lax.psum_scatter(set_part, 'row', scatter_dimension=0, tiled=True)  1210 us
    unnamed x13, waiting for transfers between devices  441 us
    psum x3, blocking collectives, shards(): gram_matrix = lax.psum(local_gram, ('row', 'col')) / total_rows  244 us
    all_gather x3, waiting for transfers between devices, shards(): set_probe = lax.all_gather(own_probe, 'row', axis=0, tiled=True)  220 us
  transfers between devices with their start and end apart: 11, of which 8 were waited for; matrix products, arithmetic and copies ran while one was open for 4% of the time, Pallas kernels for 0%

commit v1 on v0

v1 whole, which is shorter than its diff:
```python
import jax
import jax.numpy as jnp
from jax import lax
from jax.experimental import pallas as pl
from jax.experimental.pallas import tpu as pltpu
from jax.sharding import PartitionSpec as P

ITERS = 3
MESH = pl.DeviceIdType.MESH
F32 = jnp.float32
BF16 = jnp.bfloat16
HIGH = lax.Precision.HIGHEST

SLOTS = 64
BLK = 256
K = 64
BANDS = 64
CHIPS = 32
PLANE = 16
COLS = 4

ROW, COL, PREV_COL, PREV_ROW, LAST_COL, LAST_ROW = (i * SLOTS for i in range(6))


def remote(src, dst, send_sem, recv_sem, device):
    return pltpu.make_async_remote_copy(
        src_ref=src,
        dst_ref=dst,
        send_sem=send_sem,
        recv_sem=recv_sem,
        device_id=device,
        device_id_type=MESH,
    )


def nt(a, b, precision=None):
    return lax.dot_general(
        a, b, (((1,), (1,)), ((), ())), preferred_element_type=F32, precision=precision
    )


def nn(a, b, precision=None):
    return lax.dot_general(
        a, b, (((1,), (0,)), ((), ())), preferred_element_type=F32, precision=precision
    )


def loop(first, last, body):
    def step(i, carry):
        body(i)
        return carry

    lax.fori_loop(first, last, step, 0)


def inverse_factor(gram):
    row = lax.broadcasted_iota(jnp.int32, (K, 2 * K), 0)
    lane = lax.broadcasted_iota(jnp.int32, (K, 2 * K), 1)
    wide = jnp.concatenate([gram, jnp.zeros((K, K), F32)], axis=1)
    wide = wide + jnp.where(lane == row + K, 1.0, 0.0).astype(F32)
    tiles = [wide[8 * t : 8 * t + 8, :] for t in range(K // 8)]
    sub = lax.broadcasted_iota(jnp.int32, (8, 1), 0)
    for j in range(K - 1):
        t, s = divmod(j, 8)
        pivot = tiles[t][s : s + 1, :]
        scaled = pivot / pivot[:, j : j + 1]
        for u in range(t, K // 8):
            factor = tiles[u][:, j : j + 1]
            if u == t:
                if s == 7:
                    continue
                factor = jnp.where(sub > s, factor, 0.0)
            tiles[u] = tiles[u] - factor * scaled
    done = jnp.concatenate(tiles, axis=0)
    diag = jnp.sum(jnp.where(lane == row, done, 0.0), axis=1, keepdims=True)
    return done[:, K:] / jnp.sqrt(diag)


def kernel(
    idx,
    vals_hbm,
    near_hbm,
    holes,
    codes,
    out,
    vals,
    near,
    gath,
    band,
    chain_c,
    chain_f,
    deg_c,
    deg_f,
    t1,
    r1,
    t2,
    r2,
    xs,
    xr,
    wq,
    rq,
    dt1,
    dr1,
    dt2,
    dr2,
    dxs,
    dxr,
    dwq,
    drq,
    acc,
    dacc,
    basis,
    gram_send,
    gram_core,
    gram_plane,
    gram_z,
    gram_back,
    load_sem,
    g_s,
    g_r,
    c_s,
    c_r,
    x_s,
    x_r,
    f_s,
    f_r,
    b_s,
    b_r,
    t1_s,
    t1_r,
    t2_s,
    t2_r,
    z_s,
    z_r,
    q_s,
    q_r,
    a1_s,
    a1_r,
    a2_s,
    a2_r,
    a3_s,
    a3_r,
    a4_s,
    a4_r,
):
    r = lax.axis_index("row")
    c = lax.axis_index("col")
    k = r % 2
    chip = r // 2
    p = chip % PLANE
    zh = r // 32
    z = zh * COLS + c
    sib = (r + 1 - 2 * k, c)
    far = ((1 - zh) * 32 + p * 2 + k, c)

    def plane(i):
        return (zh * 32 + i * 2 + k, c)

    def in_band(i):
        return (r, i)

    def along_z(i):
        return ((i // COLS) * 32 + p * 2 + k, i % COLS)

    parts = 4
    part = SLOTS // parts
    near_load = pltpu.make_async_copy(near_hbm, near, load_sem.at[parts])
    near_load.start()
    loads = [
        pltpu.make_async_copy(
            vals_hbm.at[pl.ds(i * part, part)], vals.at[pl.ds(i * part, part)], load_sem.at[i]
        )
        for i in range(parts)
    ]
    for load in loads:
        load.start()

    barrier = pltpu.get_barrier_semaphore()
    pl.semaphore_signal(barrier, inc=1, device_id=sib, device_id_type=MESH)
    for d in range(1, PLANE):
        pl.semaphore_signal(
            barrier, inc=1, device_id=plane((p + d) % PLANE), device_id_type=MESH
        )
    for d in range(1, 2 * COLS):
        pl.semaphore_signal(
            barrier, inc=1, device_id=along_z((z + d) % (2 * COLS)), device_id_type=MESH
        )

    chain_c[0] = jnp.zeros((K, BLK), F32)
    chain_f[0] = jnp.zeros((K, BLK), F32)
    deg_c[0] = jnp.zeros((1, BLK), F32)
    deg_f[0] = jnp.zeros((1, BLK), F32)

    def mirror_send(m, chain, t1, r1, t2, r2):
        kind = t1.dtype

        def to_core(i):
            at = CHIPS - 1 - i
            t1[at] = chain[idx[LAST_COL + at * 2 + 1 - k]].astype(kind)
            remote(t1.at[at], r1.at[at], t1_s.at[m, at], t1_r.at[m, at], sib).start()

        loop(0, CHIPS - chip - k, to_core)

        def to_chip(i):
            at = CHIPS - 1 - i
            to, half = at % PLANE, at // PLANE
            remote(t1.at[at], r1.at[at], t1_s.at[m, at], t1_r.at[m, at], sib).wait_recv()
            both = (chain[idx[LAST_COL + at * 2 + k]] + r1[at].astype(F32)).astype(kind)

            @pl.when(to == p)
            def _():
                r2[PLANE + p] = both

            @pl.when(to != p)
            def _():
                t2[at] = both
                remote(
                    t2.at[at],
                    r2.at[half * PLANE + p],
                    t2_s.at[m, at],
                    t2_r.at[m, half * PLANE + p],
                    plane(to),
                ).start()

        loop(0, CHIPS - 1 - chip, to_chip)

    def mirror_cross(m, r2, t2, xs, xr):
        @pl.when(zh == 0)
        def _():
            def add(i, total):
                source = (p + i) % PLANE
                at = PLANE + source
                remote(t2.at[at], r2.at[at], t2_s.at[m, at], t2_r.at[m, at], plane(source)).wait_recv()
                return total + r2[at].astype(F32)

            xs[...] = lax.fori_loop(1, PLANE, add, r2[PLANE + p].astype(F32))
            remote(xs, xr, z_s.at[m], z_r.at[m], far).start()

    def mirror_sum(m, acc, t1, r1, t2, r2, xs, xr):
        def add(i, total):
            at = zh * PLANE + i
            remote(t2.at[at], r2.at[at], t2_s.at[m, at], t2_r.at[m, at], plane(i)).wait_recv()
            return total + r2[at].astype(F32)

        acc[...] += lax.fori_loop(0, p, add, jnp.zeros(acc.shape, F32))

        @pl.when(k == 1)
        def _():
            remote(
                t1.at[chip], r1.at[chip], t1_s.at[m, chip], t1_r.at[m, chip], sib
            ).wait_recv()
            acc[...] += r1[chip].astype(F32)

        @pl.when(zh == 1)
        def _():
            remote(xs, xr, z_s.at[m], z_r.at[m], far).wait_recv()
            acc[...] += xr[...]

    def mirror_done(m, t1, r1, t2, r2, xs, xr):
        def core_sent(i):
            at = CHIPS - 1 - i
            remote(t1.at[at], r1.at[at], t1_s.at[m, at], t1_r.at[m, at], sib).wait_send()

        loop(0, CHIPS - chip - k, core_sent)

        def chip_sent(i):
            at = CHIPS - 1 - i

            @pl.when(at % PLANE != p)
            def _():
                remote(
                    t2.at[at], r2.at[at], t2_s.at[m, at], t2_r.at[m, at], plane(at % PLANE)
                ).wait_send()

        loop(0, CHIPS - 1 - chip, chip_sent)

        @pl.when(zh == 0)
        def _():
            remote(xs, xr, z_s.at[m], z_r.at[m], far).wait_send()

    def band_send(m, wq, rq):
        for d in range(1, COLS):
            to = (c + d) % COLS
            remote(wq.at[to], rq.at[c], q_s.at[m, to], q_r.at[m, c], in_band(to)).start()

    def band_sum(m, acc, wq, rq):
        for d in range(1, COLS):
            at = (c + d) % COLS
            remote(wq.at[at], rq.at[at], q_s.at[m, at], q_r.at[m, at], in_band(at)).wait_recv()
            acc[...] += rq[at].astype(F32)

    def band_done(m, wq, rq):
        for d in range(1, COLS):
            at = (c + d) % COLS
            remote(wq.at[at], rq.at[at], q_s.at[m, at], q_r.at[m, at], in_band(at)).wait_send()

    ones = jnp.ones((8, BLK), BF16)
    for i in range(parts):
        loads[i].wait()

        def sums(s):
            deg_c[s + 1] = deg_c[idx[PREV_COL + s]] + nn(ones, vals[s])[0:1]
            deg_f[s + 1] = deg_f[idx[PREV_ROW + s]] + nt(ones, vals[s])[0:1]

        loop(i * part, (i + 1) * part, sums)
    near_load.wait()
    pl.semaphore_wait(barrier, 1 + PLANE - 1 + 2 * COLS - 1)

    mirror_send(0, deg_c, dt1, dr1, dt2, dr2)
    own_sum = jnp.zeros((1, BLK), F32)
    for q in range(COLS):
        tile = near[:, q * BLK : (q + 1) * BLK]
        own_sum = own_sum + nt(ones, tile)[0:1]
        dwq[q] = deg_f[idx[LAST_ROW + q]] + nn(ones, tile)[0:1]
    dacc[...] = own_sum + dwq[c]
    band_send(0, dwq, drq)

    hole = holes[...]
    onehot = jnp.where(
        lax.broadcasted_iota(jnp.int32, (codes.shape[0], BLK), 0) == hole, 1.0, 0.0
    ).astype(F32)
    basis[...] = lax.dot_general(
        codes[...], onehot, (((0,), (0,)), ((), ())), preferred_element_type=F32, precision=HIGH
    )

    mirror_cross(0, dr2, dt2, dxs, dxr)
    band_sum(0, dacc, dwq, drq)
    mirror_sum(0, dacc, dt1, dr1, dt2, dr2, dxs, dxr)
    mirror_done(0, dt1, dr1, dt2, dr2, dxs, dxr)
    band_done(0, dwq, drq)
    scale = 1.0 / jnp.sqrt(dacc[...])

    def gather_copy(send, recv, at, device):
        return remote(gath.at[at], gath.at[at], send, recv, device)

    def sweep(it):
        probe = (scale * basis[...]).astype(BF16)
        gath[r] = probe
        band[c] = probe

        for d in range(1, COLS):
            to = (c + d) % COLS
            remote(band.at[c], band.at[c], b_s.at[to], b_r.at[c], in_band(to)).start()

        @pl.when(zh == 1)
        def _():
            gather_copy(x_s.at[0], x_r.at[0], r, far).start()

        loop(0, p, lambda i: gather_copy(g_s.at[i], g_r.at[p], r, plane(i)).start())

        @pl.when(k == 1)
        def _():
            gather_copy(f_s.at[r], f_r.at[r], r, sib).start()

        for d in range(1, COLS):
            at = (c + d) % COLS
            remote(band.at[at], band.at[at], b_s.at[at], b_r.at[at], in_band(at)).wait_recv()

        cross = 32 + p * 2 + k

        @pl.when(zh == 0)
        def _():
            gather_copy(x_s.at[0], x_r.at[0], cross, far).wait_recv()

            def to_plane(i):
                to = (p + i) % PLANE
                gather_copy(c_s.at[to], c_r.at[p], cross, plane(to)).start()

            loop(1, PLANE, to_plane)
            gather_copy(f_s.at[cross], f_r.at[cross], cross, sib).start()

        def backward(s):
            chain_c[s + 1] = chain_c[idx[PREV_COL + s]] + nn(band[idx[ROW + s]], vals[s])

        loop(0, SLOTS, backward)
        mirror_send(1, chain_c, t1, r1, t2, r2)

        def own_pass(i):
            at = zh * 32 + i * 2 + k
            gather_copy(g_s.at[i], g_r.at[i], at, plane(i)).wait_recv()
            gather_copy(f_s.at[at], f_r.at[at], at, sib).start()

        loop(p + 1, PLANE, own_pass)

        own = jnp.zeros((K, BLK), F32)
        for q in range(COLS):
            own = own + nt(band[q], near[:, q * BLK : (q + 1) * BLK])
        acc[...] = own

        @pl.when(zh == 0)
        def _():
            def cross_pass(i):
                source = (p + i) % PLANE
                at = 32 + source * 2 + k
                gather_copy(c_s.at[source], c_r.at[source], at, plane(source)).wait_recv()
                gather_copy(f_s.at[at], f_r.at[at], at, sib).start()

            loop(1, PLANE, cross_pass)

            def cross_core(i):
                at = 32 + i * 2 + 1 - k
                gather_copy(f_s.at[at], f_r.at[at], at, sib).wait_recv()

            loop(0, PLANE, cross_core)

        def own_core(i):
            at = zh * 32 + i * 2 + 1 - k
            gather_copy(f_s.at[at], f_r.at[at], at, sib).wait_recv()

        loop(p + k, PLANE, own_core)

        def forward(s):
            chain_f[s + 1] = chain_f[idx[PREV_ROW + s]] + nt(gath[idx[COL + s]], vals[s])

        loop(0, SLOTS, forward)
        for q in range(COLS):
            total = chain_f[idx[LAST_ROW + q]] + nn(probe, near[:, q * BLK : (q + 1) * BLK])
            wq[q] = total.astype(BF16)

            @pl.when(c == q)
            def _():
                acc[...] += total

        band_send(1, wq, rq)

        @pl.when(zh == 0)
        def _():
            def plane_sent(i):
                to = (p + i) % PLANE
                gather_copy(c_s.at[to], c_r.at[p], cross, plane(to)).wait_send()

            loop(1, PLANE, plane_sent)

            def cross_sent(i):
                at = 32 + i * 2 + k
                gather_copy(f_s.at[at], f_r.at[at], at, sib).wait_send()

            loop(0, PLANE, cross_sent)

        def own_sent(i):
            at = zh * 32 + i * 2 + k
            gather_copy(f_s.at[at], f_r.at[at], at, sib).wait_send()

        loop(p + 1, PLANE, own_sent)

        mirror_cross(1, r2, t2, xs, xr)
        band_sum(1, acc, wq, rq)
        mirror_sum(1, acc, t1, r1, t2, r2, xs, xr)

        image = scale * acc[...]
        gram = nt(image, image, HIGH)

        low = jnp.concatenate([gram[0:16], gram[16:32]], axis=1)
        high = jnp.concatenate([gram[32:48], gram[48:64]], axis=1)
        gram_send[it] = jnp.where(k == 0, high, low)
        core = remote(gram_send.at[it], gram_core.at[it], a1_s.at[it], a1_r.at[it], sib)
        core.start()
        core.wait_recv()
        gram_plane[it, p] = jnp.where(k == 0, low, high) + gram_core[it]

        def plane_copy(to, source):
            return remote(
                gram_plane.at[it, source],
                gram_plane.at[it, source],
                a2_s.at[it, to],
                a2_r.at[it, source],
                plane(to if source is p else source),
            )

        def plane_start(i):
            to = (p + i) % PLANE
            plane_copy(to, p).start()

        loop(1, PLANE, plane_start)

        def plane_wait(i):
            source = (p + i) % PLANE
            plane_copy(source, source).wait_recv()

        loop(1, PLANE, plane_wait)
        total = gram_plane[it, 0]
        for i in range(1, PLANE):
            total = total + gram_plane[it, i]
        gram_z[it, z] = total
        for d in range(1, 2 * COLS):
            to = (z + d) % (2 * COLS)
            remote(
                gram_z.at[it, z], gram_z.at[it, z], a3_s.at[it, to], a3_r.at[it, z], along_z(to)
            ).start()
        for d in range(1, 2 * COLS):
            at = (z + d) % (2 * COLS)
            remote(
                gram_z.at[it, at], gram_z.at[it, at], a3_s.at[it, at], a3_r.at[it, at], along_z(at)
            ).wait_recv()
        total = gram_z[it, 0]
        for i in range(1, 2 * COLS):
            total = total + gram_z[it, i]
        gram_back[it, k] = total
        back = remote(
            gram_back.at[it, k], gram_back.at[it, k], a4_s.at[it], a4_r.at[it, k], sib
        )
        back.start()
        remote(
            gram_back.at[it, 1 - k], gram_back.at[it, 1 - k], a4_s.at[it], a4_r.at[it, 1 - k], sib
        ).wait_recv()
        low = gram_back[it, 0]
        high = gram_back[it, 1]
        gram = jnp.concatenate([low[:, :K], low[:, K:], high[:, :K], high[:, K:]], axis=0)
        total_rows = BLK * BANDS * COLS
        basis[...] = nn(inverse_factor(gram * (1.0 / total_rows)), image, HIGH)

        for d in range(1, COLS):
            to = (c + d) % COLS
            remote(band.at[c], band.at[c], b_s.at[to], b_r.at[c], in_band(to)).wait_send()

        @pl.when(zh == 1)
        def _():
            gather_copy(x_s.at[0], x_r.at[0], r, far).wait_send()

        loop(0, p, lambda i: gather_copy(g_s.at[i], g_r.at[p], r, plane(i)).wait_send())

        @pl.when(k == 1)
        def _():
            gather_copy(f_s.at[r], f_r.at[r], r, sib).wait_send()

        mirror_done(1, t1, r1, t2, r2, xs, xr)
        band_done(1, wq, rq)
        core.wait_send()

        def plane_done(i):
            to = (p + i) % PLANE
            plane_copy(to, p).wait_send()

        loop(1, PLANE, plane_done)
        for d in range(1, 2 * COLS):
            to = (z + d) % (2 * COLS)
            remote(
                gram_z.at[it, z], gram_z.at[it, z], a3_s.at[it, to], a3_r.at[it, z], along_z(to)
            ).wait_send()
        back.wait_send()

    loop(0, ITERS, sweep)
    out[...] = basis[...].T


def shards(block_rows, block_cols, block_values, near_values, hole_ids, start_codes):
    row_index = lax.axis_index("row")
    rows = block_rows.reshape(SLOTS)
    cols = block_cols.reshape(SLOTS)
    live = rows >= 0
    local_row = jnp.where(live, rows - row_index * COLS, -1)
    local_col = jnp.where(live, cols // COLS, -1)
    slot = jnp.arange(SLOTS, dtype=jnp.int32)

    def previous(keys):
        same = (keys[None, :] == keys[:, None]) & (slot[None, :] < slot[:, None])
        return jnp.max(jnp.where(same, slot[None, :] + 1, 0), axis=1)

    def last(keys):
        same = keys[None, :] == slot[:, None]
        return jnp.max(jnp.where(same, slot[None, :] + 1, 0), axis=1)

    idx = jnp.concatenate(
        [
            jnp.maximum(local_row, 0),
            jnp.maximum(local_col, 0),
            previous(local_col),
            previous(local_row),
            last(local_col),
            last(local_row),
        ]
    ).astype(jnp.int32)
    block = (K, BLK)
    line = (1, BLK)
    dma = pltpu.SemaphoreType.DMA
    return pl.pallas_call(
        kernel,
        name="subspace",
        out_shape=jax.ShapeDtypeStruct((BLK, K), F32),
        in_specs=[
            pl.BlockSpec(memory_space=pltpu.SMEM),
            pl.BlockSpec(memory_space=pl.ANY),
            pl.BlockSpec(memory_space=pl.ANY),
            pl.BlockSpec(memory_space=pltpu.VMEM),
            pl.BlockSpec(memory_space=pltpu.VMEM),
        ],
        out_specs=pl.BlockSpec(memory_space=pltpu.VMEM),
        scratch_shapes=[
            pltpu.VMEM((SLOTS, BLK, BLK), BF16),
            pltpu.VMEM((BLK, COLS * BLK), BF16),
            pltpu.VMEM((BANDS, *block), BF16),
            pltpu.VMEM((COLS, *block), BF16),
            pltpu.VMEM((SLOTS + 1, *block), F32),
            pltpu.VMEM((SLOTS + 1, *block), F32),
            pltpu.VMEM((SLOTS + 1, *line), F32),
            pltpu.VMEM((SLOTS + 1, *line), F32),
            pltpu.VMEM((CHIPS, *block), BF16),
            pltpu.VMEM((CHIPS, *block), BF16),
            pltpu.VMEM((CHIPS, *block), BF16),
            pltpu.VMEM((CHIPS, *block), BF16),
            pltpu.VMEM(block, F32),
            pltpu.VMEM(block, F32),
            pltpu.VMEM((COLS, *block), BF16),
            pltpu.VMEM((COLS, *block), BF16),
            pltpu.VMEM((CHIPS, *line), F32),
            pltpu.VMEM((CHIPS, *line), F32),
            pltpu.VMEM((CHIPS, *line), F32),
            pltpu.VMEM((CHIPS, *line), F32),
            pltpu.VMEM(line, F32),
            pltpu.VMEM(line, F32),
            pltpu.VMEM((COLS, *line), F32),
            pltpu.VMEM((COLS, *line), F32),
            pltpu.VMEM(block, F32),
            pltpu.VMEM(line, F32),
            pltpu.VMEM(block, F32),
            pltpu.VMEM((ITERS, 16, 2 * K), F32),
            pltpu.VMEM((ITERS, 16, 2 * K), F32),
            pltpu.VMEM((ITERS, PLANE, 16, 2 * K), F32),
            pltpu.VMEM((ITERS, 2 * COLS, 16, 2 * K), F32),
            pltpu.VMEM((ITERS, 2, 16, 2 * K), F32),
            dma((5,)),
            dma((PLANE,)),
            dma((PLANE,)),
            dma((PLANE,)),
            dma((PLANE,)),
            dma((1,)),
            dma((1,)),
            dma((BANDS,)),
            dma((BANDS,)),
            dma((COLS,)),
            dma((COLS,)),
            dma((2, CHIPS)),
            dma((2, CHIPS)),
            dma((2, CHIPS)),
            dma((2, CHIPS)),
            dma((2,)),
            dma((2,)),
            dma((2, COLS)),
            dma((2, COLS)),
            dma((ITERS,)),
            dma((ITERS,)),
            dma((ITERS, PLANE)),
            dma((ITERS, PLANE)),
            dma((ITERS, 2 * COLS)),
            dma((ITERS, 2 * COLS)),
            dma((ITERS,)),
            dma((ITERS, 2)),
        ],
        compiler_params=pltpu.CompilerParams(
            collective_id=0, has_side_effects=True, vmem_limit_bytes=56 << 20
        ),
    )(
        idx,
        block_values.reshape(SLOTS, BLK, BLK),
        near_values,
        hole_ids.reshape(1, BLK),
        start_codes,
    )


def solution(mesh):
    return jax.shard_map(
        shards,
        mesh=mesh,
        in_specs=(
            P("row", "col", None),
            P("row", "col", None),
            P("row", "col", None, None, None),
            P(("row", "col"), None),
            P(("row", "col")),
            P(),
        ),
        out_specs=P(("row", "col"), None),
        check_vma=False,
    )
```

time: 2400 us -> 217 us (0.09)
  waiting for transfers between devices: 1880 us -> 0 us
  blocking collectives: 277 us -> 0 us
  Pallas kernels: 0 us -> 212 us
  matrix products: 80.3 us -> 0 us
  other arithmetic: 80.1 us -> 0.9 us
  local copies, waits for them, and re-layouts: 53.2 us -> 3.86 us
    reduce_scatter x6 -> x0, waiting for transfers between devices: 1210 us -> none  [the longest x3 1210 us: products(): return lax.psum_scatter(set_part, 'row', scatter_dimension=0, tiled=True)]
    unnamed x13 -> x0, waiting for transfers between devices: 441 us -> none
    psum x3 -> x0, blocking collectives: 244 us -> none  [shards(): gram_matrix = lax.psum(local_gram, ('row', 'col')) / total_rows]
    all_gather x3 -> x0, waiting for transfers between devices: 220 us -> none  [shards(): set_probe = lax.all_gather(own_probe, 'row', axis=0, tiled=True)]
    pallas_call x0 -> x1, Pallas kernels: none -> 212 us  [shards(): pl.pallas_call(kernel, name='subspace', out_shape=jax.ShapeDtypeStruct((B...]
    dot_general x24 -> x0, matrix products: 75.1 us -> none  [the longest x4 25.6 us: products(): jnp.einsum('sij,sjk->sik', slot_vals, set_tiles[local_col], preferred_ele...]
    scatter-add x4 -> x0, other arithmetic: 41.7 us -> none  [products(): jax.ops.segment_sum(backward, local_col, num_segments=set_blocks)]
    another operation x15 -> x0, other arithmetic: 36.2 us -> none  [the longest x9 19.6 us: shards(): factor = jnp.linalg.cholesky(gram_matrix)]
  transfers between devices with their start and end apart: 11 -> 0, of which waited for: 8 -> 0; matrix products, arithmetic and copies ran while one was open for 4% -> 0% of each run, Pallas kernels for 0% -> 0%
where the time goes in v1:
time: 217 us
  Pallas kernels  212 us (98%)
  local copies, waits for them, and re-layouts  3.86 us (2%)
    pallas_call x1, Pallas kernels, shards(): pl.pallas_call(kernel, name='subspace', out_shape=jax.ShapeDtypeStruct((B...  212 us

profile of v1, /device:TPU:1, one launch (start us, length us, event | category | flops | bytes accessed | tf_op | source)
XLA Modules:
  0.0 217.0 jit_solution(2077153571064903321)
XLA Ops:
  0.0 0.7 broadcast_maximum_fusion
  0.7 0.2 select_reduce_fusion
  0.9 0.7 concatenate.3.idx
  1.6 1.6 copy.9.codes
  3.1 212.2 %subspace.1 = f32[256,64]{1,0:T(8,128)} custom-call(s32[384]{0:T(512)} %concatenate.3.idx, bf16[64,256,256]{2,1,0:T(8,128)(2,1)} %bitcast.21, bf16[256,1024]{1,0:T(8,128)(2,1)} %near_hbm.1, s32[1,256]{1,0:T(1,128)} %bitcast.22, f32[200,64]{1,0:T(8,128)} %copy.9.codes), custom_call_target="tpu_custom_call" | custom-call | tf_op jit(solution)/shard_map/subspace/pallas_call | solution.py:576
  215.4 1.6 copy.10

commit v2 on v1

--- a/solution.py
+++ b/solution.py
@@ -18,6 +18,10 @@
 CHIPS = 32
 PLANE = 16
 COLS = 4
+SIDE = 4
+HALF = K // 2
+GROUP = 32
+SUMS = 16
 
 ROW, COL, PREV_COL, PREV_ROW, LAST_COL, LAST_ROW = (i * SLOTS for i in range(6))
 
@@ -85,6 +89,10 @@
     out,
     vals,
     near,
+    raw,
+    band_raw,
+    cross_lines,
+    band_lines,
     gath,
     band,
     chain_c,
@@ -109,7 +117,7 @@
     drq,
     acc,
     dacc,
-    basis,
+    inverse,
     gram_send,
     gram_core,
     gram_plane,
@@ -122,10 +130,18 @@
     c_r,
     x_s,
     x_r,
+    c2_s,
+    c2_r,
     f_s,
     f_r,
     b_s,
     b_r,
+    lb_s,
+    lb_r,
+    lx_s,
+    lx_r,
+    lc_s,
+    lc_r,
     t1_s,
     t1_r,
     t2_s,
@@ -148,6 +164,8 @@
     k = r % 2
     chip = r // 2
     p = chip % PLANE
+    y = p // SIDE
+    x = p % SIDE
     zh = r // 32
     z = zh * COLS + c
     sib = (r + 1 - 2 * k, c)
@@ -191,18 +209,26 @@
     deg_c[0] = jnp.zeros((1, BLK), F32)
     deg_f[0] = jnp.zeros((1, BLK), F32)
 
-    def mirror_send(m, chain, t1, r1, t2, r2):
+    def each_later(body, first):
+        @pl.when(zh == 0)
+        def _():
+            loop(1, PLANE + 1, lambda i: body(PLANE + (p + i) % PLANE))
+
+        loop(first, PLANE, lambda i: body(zh * PLANE + i))
+
+    def mirror_core(m, chain, t1, r1):
         kind = t1.dtype
 
-        def to_core(i):
-            at = CHIPS - 1 - i
+        def to_core(at):
             t1[at] = chain[idx[LAST_COL + at * 2 + 1 - k]].astype(kind)
             remote(t1.at[at], r1.at[at], t1_s.at[m, at], t1_r.at[m, at], sib).start()
 
-        loop(0, CHIPS - chip - k, to_core)
-
-        def to_chip(i):
-            at = CHIPS - 1 - i
+        each_later(to_core, p + k)
+
+    def mirror_plane(m, chain, t1, r1, t2, r2):
+        kind = t2.dtype
+
+        def to_chip(at):
             to, half = at % PLANE, at // PLANE
             remote(t1.at[at], r1.at[at], t1_s.at[m, at], t1_r.at[m, at], sib).wait_recv()
             both = (chain[idx[LAST_COL + at * 2 + k]] + r1[at].astype(F32)).astype(kind)
@@ -222,7 +248,7 @@
                     plane(to),
                 ).start()
 
-        loop(0, CHIPS - 1 - chip, to_chip)
+        each_later(to_chip, p + 1)
 
     def mirror_cross(m, r2, t2, xs, xr):
         @pl.when(zh == 0)
@@ -294,19 +320,189 @@
             at = (c + d) % COLS
             remote(wq.at[at], rq.at[at], q_s.at[m, at], q_r.at[m, at], in_band(at)).wait_send()
 
+    cross = 32 + p * 2 + k
+    place = (x, y)
+
+    def line_of(half, i):
+        return y * SIDE + i if half == 0 else i * SIDE + x
+
+    def gather_copy(n, send, recv, at, device):
+        block = gath.at[at]
+        return remote(block, block, send, recv, device)
+
+    def half_copy(n, half, send, recv, at, device):
+        block = raw.at[n, at, pl.ds(half * HALF, HALF)]
+        return remote(block, block, send, recv, device)
+
+    def first_copy(n, half, i, source, device):
+        at = line_of(half, source)
+        return half_copy(n, half, c_s.at[n, half, i], c_r.at[n, half, source], at, plane(device))
+
+    def second_copy(n, half, e, d):
+        source = line_of(half, (place[half] + e) % SIDE)
+        to = line_of(1 - half, (place[1 - half] + d) % SIDE)
+        return half_copy(
+            n, half, c2_s.at[n, half, e, d], c2_r.at[n, half, source], source, plane(to)
+        )
+
+    def band_copy(n, to, source, device):
+        block = band_raw.at[n, source]
+        return remote(block, block, b_s.at[n, to], b_r.at[n, source], in_band(device))
+
+    def far_copy(n):
+        return remote(band_raw.at[n, c], raw.at[n, p], x_s.at[n], x_r.at[n], far)
+
+    def own_copy(n, to, source, at, device):
+        return gather_copy(n, g_s.at[n, to], g_r.at[n, source], at, plane(device))
+
+    def core_copy(n, at):
+        return gather_copy(n, f_s.at[n, at], f_r.at[n, at], at, sib)
+
+    def gather_far(n):
+        @pl.when(zh == 1)
+        def _():
+            far_copy(n).start()
+
+    def gather_band(n):
+        for d in range(1, COLS):
+            to = (c + d) % COLS
+            band_copy(n, to, c, to).start()
+
+    def gather_own(n):
+        loop(1, p + 1, lambda i: own_copy(n, p - i, p, r, p - i).start())
+
+        @pl.when(k == 1)
+        def _():
+            core_copy(n, r).start()
+
+    def probe_of(line, block):
+        return (line * nn(inverse[...], block, HIGH)).astype(BF16)
+
+    def gather_first(n):
+        @pl.when(zh == 0)
+        def _():
+            far_copy(n).wait_recv()
+            for half in range(2):
+                for d in range(1, SIDE):
+                    to = (place[half] + d) % SIDE
+                    first_copy(n, half, to, place[half], line_of(half, to)).start()
+            for half in range(2):
+                for d in range(1, SIDE):
+                    second_copy(n, half, 0, d).start()
+
+    def gather_second(n):
+        @pl.when(zh == 0)
+        def _():
+            for e in range(1, SIDE):
+                for half in range(2):
+                    source = (place[half] + e) % SIDE
+                    first_copy(n, half, source, source, line_of(half, source)).wait_recv()
+                    for d in range(1, SIDE):
+                        second_copy(n, half, e, d).start()
+
+    def pass_own(n):
+        def own_pass(i):
+            at = zh * 32 + i * 2 + k
+            own_copy(n, i, i, at, i).wait_recv()
+            core_copy(n, at).start()
+
+        loop(p + 1, PLANE, own_pass)
+
+    def pass_cross(n):
+        @pl.when(zh == 0)
+        def _():
+            def cross_pass(i):
+                source = (p + i) % PLANE
+                at = 32 + source * 2 + k
+                for half, same in ((0, source // SIDE == y), (1, source % SIDE == x)):
+
+                    @pl.when(jnp.logical_not(same))
+                    def _():
+                        half_copy(
+                            n,
+                            half,
+                            c2_s.at[n, half, 0, 0],
+                            c2_r.at[n, half, source],
+                            source,
+                            plane(source),
+                        ).wait_recv()
+
+                gath[at] = probe_of(cross_lines[source], raw[n, source])
+                core_copy(n, at).start()
+
+            loop(0, PLANE, cross_pass)
+
+    def gather_wait(n):
+        loop(p + k, PLANE, lambda i: core_copy(n, zh * 32 + i * 2 + 1 - k).wait_recv())
+
+        @pl.when(zh == 0)
+        def _():
+            loop(0, PLANE, lambda i: core_copy(n, 32 + i * 2 + 1 - k).wait_recv())
+
+    def gather_z_done(n):
+        for d in range(1, COLS):
+            to = (c + d) % COLS
+            band_copy(n, to, c, to).wait_send()
+
+        @pl.when(zh == 1)
+        def _():
+            far_copy(n).wait_send()
+
+        @pl.when(zh == 0)
+        def _():
+            for half in range(2):
+                for d in range(1, SIDE):
+                    to = (place[half] + d) % SIDE
+                    first_copy(n, half, to, place[half], line_of(half, to)).wait_send()
+                    for e in range(SIDE):
+                        second_copy(n, half, e, d).wait_send()
+
+    def gather_done(n):
+        loop(0, p, lambda i: own_copy(n, i, p, r, i).wait_send())
+
+        @pl.when(k == 1)
+        def _():
+            core_copy(n, r).wait_send()
+
+        loop(p + 1, PLANE, lambda i: core_copy(n, zh * 32 + i * 2 + k).wait_send())
+
+        @pl.when(zh == 0)
+        def _():
+            loop(0, PLANE, lambda i: core_copy(n, 32 + i * 2 + k).wait_send())
+
+    hole = holes[...]
+    onehot = jnp.where(
+        lax.broadcasted_iota(jnp.int32, (codes.shape[0], BLK), 0) == hole, 1.0, 0.0
+    ).astype(F32)
+    start = lax.dot_general(
+        codes[...], onehot, (((0,), (0,)), ((), ())), preferred_element_type=F32, precision=HIGH
+    )
+    band_raw[0, c] = start
+    inverse[...] = jnp.where(
+        lax.broadcasted_iota(jnp.int32, (K, K), 0) == lax.broadcasted_iota(jnp.int32, (K, K), 1),
+        1.0,
+        0.0,
+    ).astype(F32)
+    pl.semaphore_wait(barrier, 1 + PLANE - 1 + 2 * COLS - 1)
+    gather_far(0)
+    gather_band(0)
+
     ones = jnp.ones((8, BLK), BF16)
     for i in range(parts):
         loads[i].wait()
 
-        def sums(s):
-            deg_c[s + 1] = deg_c[idx[PREV_COL + s]] + nn(ones, vals[s])[0:1]
-            deg_f[s + 1] = deg_f[idx[PREV_ROW + s]] + nt(ones, vals[s])[0:1]
-
-        loop(i * part, (i + 1) * part, sums)
+        def sums(g):
+            slots = [g * SUMS + u for u in range(SUMS)]
+            down = [nn(ones, vals[s])[0:1] for s in slots]
+            across = [nt(ones, vals[s])[0:1] for s in slots]
+            for u, s in enumerate(slots):
+                deg_c[s + 1] = deg_c[idx[PREV_COL + s]] + down[u]
+                deg_f[s + 1] = deg_f[idx[PREV_ROW + s]] + across[u]
+
+        loop(i * part // SUMS, (i + 1) * part // SUMS, sums)
     near_load.wait()
-    pl.semaphore_wait(barrier, 1 + PLANE - 1 + 2 * COLS - 1)
-
-    mirror_send(0, deg_c, dt1, dr1, dt2, dr2)
+
+    mirror_core(0, deg_c, dt1, dr1)
     own_sum = jnp.zeros((1, BLK), F32)
     for q in range(COLS):
         tile = near[:, q * BLK : (q + 1) * BLK]
@@ -314,105 +510,99 @@
         dwq[q] = deg_f[idx[LAST_ROW + q]] + nn(ones, tile)[0:1]
     dacc[...] = own_sum + dwq[c]
     band_send(0, dwq, drq)
-
-    hole = holes[...]
-    onehot = jnp.where(
-        lax.broadcasted_iota(jnp.int32, (codes.shape[0], BLK), 0) == hole, 1.0, 0.0
-    ).astype(F32)
-    basis[...] = lax.dot_general(
-        codes[...], onehot, (((0,), (0,)), ((), ())), preferred_element_type=F32, precision=HIGH
-    )
-
+    mirror_plane(0, deg_c, dt1, dr1, dt2, dr2)
+    gather_first(0)
     mirror_cross(0, dr2, dt2, dxs, dxr)
+    gather_second(0)
     band_sum(0, dacc, dwq, drq)
     mirror_sum(0, dacc, dt1, dr1, dt2, dr2, dxs, dxr)
+    scale = 1.0 / jnp.sqrt(dacc[...])
+
+    def line_far():
+        return remote(band_lines.at[c], cross_lines.at[p], lx_s.at[0], lx_r.at[0], far)
+
+    def line_band(to, source, device):
+        block = band_lines.at[source]
+        return remote(block, block, lb_s.at[to], lb_r.at[source], in_band(device))
+
+    band_lines[c] = scale
+    for d in range(1, COLS):
+        to = (c + d) % COLS
+        line_band(to, c, to).start()
+
+    @pl.when(zh == 1)
+    def _():
+        line_far().start()
+
     mirror_done(0, dt1, dr1, dt2, dr2, dxs, dxr)
     band_done(0, dwq, drq)
-    scale = 1.0 / jnp.sqrt(dacc[...])
-
-    def gather_copy(send, recv, at, device):
-        return remote(gath.at[at], gath.at[at], send, recv, device)
+    for d in range(1, COLS):
+        at = (c + d) % COLS
+        line_band(at, at, at).wait_recv()
+
+    def line_plane(to, source, device):
+        block = cross_lines.at[source]
+        return remote(block, block, lc_s.at[to], lc_r.at[source], plane(device))
+
+    @pl.when(zh == 0)
+    def _():
+        line_far().wait_recv()
+
+        def to_plane(i):
+            to = (p + i) % PLANE
+            line_plane(to, p, to).start()
+
+        loop(1, PLANE, to_plane)
+
+    def lines_wait():
+        @pl.when(zh == 0)
+        def _():
+            def arrived(i):
+                source = (p + i) % PLANE
+                line_plane(source, source, source).wait_recv()
+
+            loop(1, PLANE, arrived)
 
     def sweep(it):
-        probe = (scale * basis[...]).astype(BF16)
-        gath[r] = probe
-        band[c] = probe
-
-        for d in range(1, COLS):
-            to = (c + d) % COLS
-            remote(band.at[c], band.at[c], b_s.at[to], b_r.at[c], in_band(to)).start()
-
-        @pl.when(zh == 1)
-        def _():
-            gather_copy(x_s.at[0], x_r.at[0], r, far).start()
-
-        loop(0, p, lambda i: gather_copy(g_s.at[i], g_r.at[p], r, plane(i)).start())
-
-        @pl.when(k == 1)
-        def _():
-            gather_copy(f_s.at[r], f_r.at[r], r, sib).start()
-
         for d in range(1, COLS):
             at = (c + d) % COLS
-            remote(band.at[at], band.at[at], b_s.at[at], b_r.at[at], in_band(at)).wait_recv()
-
-        cross = 32 + p * 2 + k
-
-        @pl.when(zh == 0)
-        def _():
-            gather_copy(x_s.at[0], x_r.at[0], cross, far).wait_recv()
-
-            def to_plane(i):
-                to = (p + i) % PLANE
-                gather_copy(c_s.at[to], c_r.at[p], cross, plane(to)).start()
-
-            loop(1, PLANE, to_plane)
-            gather_copy(f_s.at[cross], f_r.at[cross], cross, sib).start()
-
-        def backward(s):
-            chain_c[s + 1] = chain_c[idx[PREV_COL + s]] + nn(band[idx[ROW + s]], vals[s])
-
-        loop(0, SLOTS, backward)
-        mirror_send(1, chain_c, t1, r1, t2, r2)
-
-        def own_pass(i):
-            at = zh * 32 + i * 2 + k
-            gather_copy(g_s.at[i], g_r.at[i], at, plane(i)).wait_recv()
-            gather_copy(f_s.at[at], f_r.at[at], at, sib).start()
-
-        loop(p + 1, PLANE, own_pass)
+            band_copy(it, at, at, at).wait_recv()
+        for q in range(COLS):
+            band[q] = probe_of(band_lines[q], band_raw[it, q])
+        gath[r] = band[c]
+        gather_own(it)
+
+        def backward(g):
+            slots = [g * GROUP + u for u in range(GROUP)]
+            tiles = [nn(band[idx[ROW + s]], vals[s]) for s in slots]
+            for s, tile in zip(slots, tiles):
+                chain_c[s + 1] = chain_c[idx[PREV_COL + s]] + tile
+
+        loop(0, SLOTS // GROUP, backward)
+        mirror_core(1, chain_c, t1, r1)
 
         own = jnp.zeros((K, BLK), F32)
         for q in range(COLS):
             own = own + nt(band[q], near[:, q * BLK : (q + 1) * BLK])
         acc[...] = own
 
-        @pl.when(zh == 0)
-        def _():
-            def cross_pass(i):
-                source = (p + i) % PLANE
-                at = 32 + source * 2 + k
-                gather_copy(c_s.at[source], c_r.at[source], at, plane(source)).wait_recv()
-                gather_copy(f_s.at[at], f_r.at[at], at, sib).start()
-
-            loop(1, PLANE, cross_pass)
-
-            def cross_core(i):
-                at = 32 + i * 2 + 1 - k
-                gather_copy(f_s.at[at], f_r.at[at], at, sib).wait_recv()
-
-            loop(0, PLANE, cross_core)
-
-        def own_core(i):
-            at = zh * 32 + i * 2 + 1 - k
-            gather_copy(f_s.at[at], f_r.at[at], at, sib).wait_recv()
-
-        loop(p + k, PLANE, own_core)
-
-        def forward(s):
-            chain_f[s + 1] = chain_f[idx[PREV_ROW + s]] + nt(gath[idx[COL + s]], vals[s])
-
-        loop(0, SLOTS, forward)
+        mirror_plane(1, chain_c, t1, r1, t2, r2)
+
+        pass_own(it)
+        pl.when(it == 0)(lines_wait)
+        pass_cross(it)
+        gather_wait(it)
+
+        mirror_cross(1, r2, t2, xs, xr)
+
+        def forward(g):
+            slots = [g * GROUP + u for u in range(GROUP)]
+            tiles = [nt(gath[idx[COL + s]], vals[s]) for s in slots]
+            for s, tile in zip(slots, tiles):
+                chain_f[s + 1] = chain_f[idx[PREV_ROW + s]] + tile
+
+        loop(0, SLOTS // GROUP, forward)
+        probe = band[c]
         for q in range(COLS):
             total = chain_f[idx[LAST_ROW + q]] + nn(probe, near[:, q * BLK : (q + 1) * BLK])
             wq[q] = total.astype(BF16)
@@ -422,32 +612,21 @@
                 acc[...] += total
 
         band_send(1, wq, rq)
-
-        @pl.when(zh == 0)
-        def _():
-            def plane_sent(i):
-                to = (p + i) % PLANE
-                gather_copy(c_s.at[to], c_r.at[p], cross, plane(to)).wait_send()
-
-            loop(1, PLANE, plane_sent)
-
-            def cross_sent(i):
-                at = 32 + i * 2 + k
-                gather_copy(f_s.at[at], f_r.at[at], at, sib).wait_send()
-
-            loop(0, PLANE, cross_sent)
-
-        def own_sent(i):
-            at = zh * 32 + i * 2 + k
-            gather_copy(f_s.at[at], f_r.at[at], at, sib).wait_send()
-
-        loop(p + 1, PLANE, own_sent)
-
-        mirror_cross(1, r2, t2, xs, xr)
+        gather_done(it)
         band_sum(1, acc, wq, rq)
         mirror_sum(1, acc, t1, r1, t2, r2, xs, xr)
 
         image = scale * acc[...]
+        more = it < ITERS - 1
+
+        @pl.when(more)
+        def _():
+            band_raw[it + 1, c] = image
+            gather_far(it + 1)
+
+        def when_more(stage):
+            pl.when(more)(lambda: stage(it + 1))
+
         gram = nt(image, image, HIGH)
 
         low = jnp.concatenate([gram[0:16], gram[16:32]], axis=1)
@@ -458,70 +637,59 @@
         core.wait_recv()
         gram_plane[it, p] = jnp.where(k == 0, low, high) + gram_core[it]
 
-        def plane_copy(to, source):
-            return remote(
-                gram_plane.at[it, source],
-                gram_plane.at[it, source],
-                a2_s.at[it, to],
-                a2_r.at[it, source],
-                plane(to if source is p else source),
-            )
+        def plane_copy(to, source, device):
+            block = gram_plane.at[it, source]
+            return remote(block, block, a2_s.at[it, to], a2_r.at[it, source], plane(device))
 
         def plane_start(i):
             to = (p + i) % PLANE
-            plane_copy(to, p).start()
+            plane_copy(to, p, to).start()
 
         loop(1, PLANE, plane_start)
 
         def plane_wait(i):
             source = (p + i) % PLANE
-            plane_copy(source, source).wait_recv()
+            plane_copy(source, source, source).wait_recv()
 
         loop(1, PLANE, plane_wait)
         total = gram_plane[it, 0]
         for i in range(1, PLANE):
             total = total + gram_plane[it, i]
         gram_z[it, z] = total
+
+        def z_copy(to, source, device):
+            block = gram_z.at[it, source]
+            return remote(block, block, a3_s.at[it, to], a3_r.at[it, source], along_z(device))
+
         for d in range(1, 2 * COLS):
             to = (z + d) % (2 * COLS)
-            remote(
-                gram_z.at[it, z], gram_z.at[it, z], a3_s.at[it, to], a3_r.at[it, z], along_z(to)
-            ).start()
+            z_copy(to, z, to).start()
+        when_more(gather_band)
+        when_more(gather_first)
         for d in range(1, 2 * COLS):
             at = (z + d) % (2 * COLS)
-            remote(
-                gram_z.at[it, at], gram_z.at[it, at], a3_s.at[it, at], a3_r.at[it, at], along_z(at)
-            ).wait_recv()
+            z_copy(at, at, at).wait_recv()
         total = gram_z[it, 0]
         for i in range(1, 2 * COLS):
             total = total + gram_z[it, i]
         gram_back[it, k] = total
-        back = remote(
-            gram_back.at[it, k], gram_back.at[it, k], a4_s.at[it], a4_r.at[it, k], sib
-        )
-        back.start()
-        remote(
-            gram_back.at[it, 1 - k], gram_back.at[it, 1 - k], a4_s.at[it], a4_r.at[it, 1 - k], sib
-        ).wait_recv()
+
+        def back_copy(half):
+            block = gram_back.at[it, half]
+            return remote(block, block, a4_s.at[it], a4_r.at[it, half], sib)
+
+        back_copy(k).start()
+        when_more(gather_second)
+        back_copy(1 - k).wait_recv()
         low = gram_back[it, 0]
         high = gram_back[it, 1]
         gram = jnp.concatenate([low[:, :K], low[:, K:], high[:, :K], high[:, K:]], axis=0)
         total_rows = BLK * BANDS * COLS
-        basis[...] = nn(inverse_factor(gram * (1.0 / total_rows)), image, HIGH)
-
-        for d in range(1, COLS):
-            to = (c + d) % COLS
-            remote(band.at[c], band.at[c], b_s.at[to], b_r.at[c], in_band(to)).wait_send()
-
-        @pl.when(zh == 1)
-        def _():
-            gather_copy(x_s.at[0], x_r.at[0], r, far).wait_send()
-
-        loop(0, p, lambda i: gather_copy(g_s.at[i], g_r.at[p], r, plane(i)).wait_send())
-
-        @pl.when(k == 1)
-        def _():
-            gather_copy(f_s.at[r], f_r.at[r], r, sib).wait_send()
+        inverse[...] = inverse_factor(gram * (1.0 / total_rows))
+
+        @pl.when(it == ITERS - 1)
+        def _():
+            out[...] = nn(inverse[...], image, HIGH).T
 
         mirror_done(1, t1, r1, t2, r2, xs, xr)
         band_done(1, wq, rq)
@@ -529,18 +697,31 @@
 
         def plane_done(i):
             to = (p + i) % PLANE
-            plane_copy(to, p).wait_send()
+            plane_copy(to, p, to).wait_send()
 
         loop(1, PLANE, plane_done)
         for d in range(1, 2 * COLS):
             to = (z + d) % (2 * COLS)
-            remote(
-                gram_z.at[it, z], gram_z.at[it, z], a3_s.at[it, to], a3_r.at[it, z], along_z(to)
-            ).wait_send()
-        back.wait_send()
+            z_copy(to, z, to).wait_send()
+        back_copy(k).wait_send()
+        gather_z_done(it)
 
     loop(0, ITERS, sweep)
-    out[...] = basis[...].T
+    for d in range(1, COLS):
+        to = (c + d) % COLS
+        line_band(to, c, to).wait_send()
+
+    @pl.when(zh == 1)
+    def _():
+        line_far().wait_send()
+
+    @pl.when(zh == 0)
+    def _():
+        def line_sent(i):
+            to = (p + i) % PLANE
+            line_plane(to, p, to).wait_send()
+
+        loop(1, PLANE, line_sent)
 
 
 def shards(block_rows, block_cols, block_values, near_values, hole_ids, start_codes):
@@ -588,6 +769,10 @@
         scratch_shapes=[
             pltpu.VMEM((SLOTS, BLK, BLK), BF16),
             pltpu.VMEM((BLK, COLS * BLK), BF16),
+            pltpu.VMEM((ITERS, PLANE, *block), F32),
+            pltpu.VMEM((ITERS, COLS, *block), F32),
+            pltpu.VMEM((PLANE, *line), F32),
+            pltpu.VMEM((COLS, *line), F32),
             pltpu.VMEM((BANDS, *block), BF16),
             pltpu.VMEM((COLS, *block), BF16),
             pltpu.VMEM((SLOTS + 1, *block), F32),
@@ -612,23 +797,31 @@
             pltpu.VMEM((COLS, *line), F32),
             pltpu.VMEM(block, F32),
             pltpu.VMEM(line, F32),
-            pltpu.VMEM(block, F32),
+            pltpu.VMEM((K, K), F32),
             pltpu.VMEM((ITERS, 16, 2 * K), F32),
             pltpu.VMEM((ITERS, 16, 2 * K), F32),
             pltpu.VMEM((ITERS, PLANE, 16, 2 * K), F32),
             pltpu.VMEM((ITERS, 2 * COLS, 16, 2 * K), F32),
             pltpu.VMEM((ITERS, 2, 16, 2 * K), F32),
             dma((5,)),
+            dma((ITERS, PLANE)),
+            dma((ITERS, PLANE)),
+            dma((ITERS, 2, SIDE)),
+            dma((ITERS, 2, SIDE)),
+            dma((ITERS,)),
+            dma((ITERS,)),
+            dma((ITERS, 2, SIDE, SIDE)),
+            dma((ITERS, 2, PLANE)),
+            dma((ITERS, BANDS)),
+            dma((ITERS, BANDS)),
+            dma((ITERS, COLS)),
+            dma((ITERS, COLS)),
+            dma((COLS,)),
+            dma((COLS,)),
+            dma((1,)),
+            dma((1,)),
             dma((PLANE,)),
             dma((PLANE,)),
-            dma((PLANE,)),
-            dma((PLANE,)),
-            dma((1,)),
-            dma((1,)),
-            dma((BANDS,)),
-            dma((BANDS,)),
-            dma((COLS,)),
-            dma((COLS,)),
             dma((2, CHIPS)),
             dma((2, CHIPS)),
             dma((2, CHIPS)),

time: 217 us -> 176 us (0.81)
  Pallas kernels: 212 us -> 171 us
    pallas_call x1, Pallas kernels: 212 us -> 171 us  [shards(): pl.pallas_call(kernel, name='subspace', out_shape=jax.ShapeDtypeStruct((B...]
where the time goes in v2:
time: 176 us
  Pallas kernels  171 us (97%)
  local copies, waits for them, and re-layouts  3.86 us (2%)
    pallas_call x1, Pallas kernels, shards(): pl.pallas_call(kernel, name='subspace', out_shape=jax.ShapeDtypeStruct((B...  171 us

profile of v2, /device:TPU:1, one launch (start us, length us, event | category | flops | bytes accessed | tf_op | source)
XLA Modules:
  0.0 175.6 jit_solution(3383758071472099556)
XLA Ops:
  0.0 0.7 broadcast_maximum_fusion
  0.7 0.2 select_reduce_fusion
  0.9 0.7 concatenate.3.idx
  1.6 1.6 copy.9.codes
  3.1 170.8 %subspace.1 = f32[256,64]{1,0:T(8,128)} custom-call(s32[384]{0:T(512)} %concatenate.3.idx, bf16[64,256,256]{2,1,0:T(8,128)(2,1)} %bitcast.21, bf16[256,1024]{1,0:T(8,128)(2,1)} %near_hbm.1, s32[1,256]{1,0:T(1,128)} %bitcast.22, f32[200,64]{1,0:T(8,128)} %copy.9.codes), custom_call_target="tpu_custom_call" | custom-call | tf_op jit(solution)/shard_map/subspace/pallas_call | solution.py:757
  174.0 1.6 copy.10

commit v3 on v2

--- a/solution.py
+++ b/solution.py
@@ -20,6 +20,7 @@
 COLS = 4
 SIDE = 4
 HALF = K // 2
+TILE = 8
 GROUP = 32
 SUMS = 16
 
@@ -60,21 +61,41 @@
 def inverse_factor(gram):
     row = lax.broadcasted_iota(jnp.int32, (K, 2 * K), 0)
     lane = lax.broadcasted_iota(jnp.int32, (K, 2 * K), 1)
+    sub = lax.broadcasted_iota(jnp.int32, (TILE, 2 * K), 0)
     wide = jnp.concatenate([gram, jnp.zeros((K, K), F32)], axis=1)
     wide = wide + jnp.where(lane == row + K, 1.0, 0.0).astype(F32)
-    tiles = [wide[8 * t : 8 * t + 8, :] for t in range(K // 8)]
-    sub = lax.broadcasted_iota(jnp.int32, (8, 1), 0)
-    for j in range(K - 1):
-        t, s = divmod(j, 8)
-        pivot = tiles[t][s : s + 1, :]
-        scaled = pivot / pivot[:, j : j + 1]
-        for u in range(t, K // 8):
-            factor = tiles[u][:, j : j + 1]
-            if u == t:
-                if s == 7:
-                    continue
-                factor = jnp.where(sub > s, factor, 0.0)
-            tiles[u] = tiles[u] - factor * scaled
+    tiles = [wide[t : t + TILE, :] for t in range(0, K, TILE)]
+    for t, tile in enumerate(tiles):
+        first = t * TILE
+        rows = [tile[i : i + 1, :] for i in range(TILE)]
+        entry = {
+            (i, m): jnp.broadcast_to(rows[i][:, first + m : first + m + 1], (1, 2 * K))
+            for i in range(TILE)
+            for m in range(i, TILE)
+        }
+        later = range(t + 1, K // TILE)
+        factor = {
+            (u, m): jnp.broadcast_to(tiles[u][:, first + m : first + m + 1], (TILE, 2 * K))
+            for u in later
+            for m in range(TILE)
+        }
+        scaled = []
+        for i in range(TILE):
+            reciprocal = 1.0 / entry[i, i]
+            for n in range(i + 1, TILE):
+                ratio = entry[i, n] * reciprocal
+                rows[n] = rows[n] - ratio * rows[i]
+                for m in range(n, TILE):
+                    entry[n, m] = entry[n, m] - ratio * entry[i, m]
+                for u in later:
+                    factor[u, n] = factor[u, n] - ratio * factor[u, i]
+            scaled.append(rows[i] * reciprocal)
+        for u in later:
+            for i in range(TILE):
+                tiles[u] = tiles[u] - factor[u, i] * scaled[i]
+        for i in range(1, TILE):
+            tile = jnp.where(sub == i, rows[i], tile)
+        tiles[t] = tile
     done = jnp.concatenate(tiles, axis=0)
     diag = jnp.sum(jnp.where(lane == row, done, 0.0), axis=1, keepdims=True)
     return done[:, K:] / jnp.sqrt(diag)
@@ -113,6 +134,9 @@
     dr2,
     dxs,
     dxr,
+    code_parts,
+    hole_band,
+    hole_cross,
     dwq,
     drq,
     acc,
@@ -142,6 +166,12 @@
     lx_r,
     lc_s,
     lc_r,
+    hb_s,
+    hb_r,
+    hx_s,
+    hx_r,
+    hc_s,
+    hc_r,
     t1_s,
     t1_r,
     t2_s,
@@ -416,7 +446,7 @@
                 at = 32 + source * 2 + k
                 for half, same in ((0, source // SIDE == y), (1, source % SIDE == x)):
 
-                    @pl.when(jnp.logical_not(same))
+                    @pl.when(jnp.logical_and(n > 0, jnp.logical_not(same)))
                     def _():
                         half_copy(
                             n,
@@ -470,22 +500,37 @@
         def _():
             loop(0, PLANE, lambda i: core_copy(n, 32 + i * 2 + k).wait_send())
 
-    hole = holes[...]
-    onehot = jnp.where(
-        lax.broadcasted_iota(jnp.int32, (codes.shape[0], BLK), 0) == hole, 1.0, 0.0
-    ).astype(F32)
-    start = lax.dot_general(
-        codes[...], onehot, (((0,), (0,)), ((), ())), preferred_element_type=F32, precision=HIGH
-    )
-    band_raw[0, c] = start
+    code_high = codes[...].astype(BF16)
+    code_rest = codes[...] - code_high.astype(F32)
+    code_middle = code_rest.astype(BF16)
+    code_low = (code_rest - code_middle.astype(F32)).astype(BF16)
+    code_parts[...] = jnp.concatenate([code_high, code_middle, code_low], axis=0)
+
+    def start_of(hole):
+        onehot = jnp.where(
+            lax.broadcasted_iota(jnp.int32, (codes.shape[1], BLK), 0) == hole, 1.0, 0.0
+        ).astype(BF16)
+        picked = nn(code_parts[...], onehot)
+        return picked[:K] + picked[K : 2 * K] + picked[2 * K :]
+
+    def hole_band_copy(to, source, device):
+        return remote(
+            holes, hole_band.at[source], hb_s.at[to], hb_r.at[source], in_band(device)
+        )
+
+    def hole_far_copy():
+        return remote(holes, hole_cross.at[p], hx_s.at[0], hx_r.at[0], far)
+
+    def hole_plane_copy(to, source, device):
+        block = hole_cross.at[source]
+        return remote(block, block, hc_s.at[to], hc_r.at[source], plane(device))
+
+    band_raw[0, c] = start_of(holes[...])
     inverse[...] = jnp.where(
         lax.broadcasted_iota(jnp.int32, (K, K), 0) == lax.broadcasted_iota(jnp.int32, (K, K), 1),
         1.0,
         0.0,
     ).astype(F32)
-    pl.semaphore_wait(barrier, 1 + PLANE - 1 + 2 * COLS - 1)
-    gather_far(0)
-    gather_band(0)
 
     ones = jnp.ones((8, BLK), BF16)
     for i in range(parts):
@@ -501,6 +546,15 @@
 
         loop(i * part // SUMS, (i + 1) * part // SUMS, sums)
     near_load.wait()
+    pl.semaphore_wait(barrier, 1 + PLANE - 1 + 2 * COLS - 1)
+    for d in range(1, COLS):
+        to = (c + d) % COLS
+        hole_band_copy(to, c, to).start()
+
+    @pl.when(zh == 1)
+    def _():
+        hole_far_copy().start()
+
 
     mirror_core(0, deg_c, dt1, dr1)
     own_sum = jnp.zeros((1, BLK), F32)
@@ -511,9 +565,22 @@
     dacc[...] = own_sum + dwq[c]
     band_send(0, dwq, drq)
     mirror_plane(0, deg_c, dt1, dr1, dt2, dr2)
-    gather_first(0)
+
+    @pl.when(zh == 0)
+    def _():
+        hole_far_copy().wait_recv()
+
+        def hole_start(i):
+            to = (p + i) % PLANE
+            hole_plane_copy(to, p, to).start()
+
+        loop(1, PLANE, hole_start)
+
+    for d in range(1, COLS):
+        at = (c + d) % COLS
+        hole_band_copy(at, at, at).wait_recv()
+        band_raw[0, at] = start_of(hole_band[at])
     mirror_cross(0, dr2, dt2, dxs, dxr)
-    gather_second(0)
     band_sum(0, dacc, dwq, drq)
     mirror_sum(0, dacc, dt1, dr1, dt2, dr2, dxs, dxr)
     scale = 1.0 / jnp.sqrt(dacc[...])
@@ -533,6 +600,17 @@
     @pl.when(zh == 1)
     def _():
         line_far().start()
+
+    @pl.when(zh == 0)
+    def _():
+        raw[0, p] = start_of(hole_cross[p])
+
+        def hole_wait(i):
+            source = (p + i) % PLANE
+            hole_plane_copy(source, source, source).wait_recv()
+            raw[0, source] = start_of(hole_cross[source])
+
+        loop(1, PLANE, hole_wait)
 
     mirror_done(0, dt1, dr1, dt2, dr2, dxs, dxr)
     band_done(0, dwq, drq)
@@ -564,9 +642,12 @@
             loop(1, PLANE, arrived)
 
     def sweep(it):
-        for d in range(1, COLS):
-            at = (c + d) % COLS
-            band_copy(it, at, at, at).wait_recv()
+        @pl.when(it > 0)
+        def _():
+            for d in range(1, COLS):
+                at = (c + d) % COLS
+                band_copy(it, at, at, at).wait_recv()
+
         for q in range(COLS):
             band[q] = probe_of(band_lines[q], band_raw[it, q])
         gath[r] = band[c]
@@ -689,7 +770,7 @@
 
         @pl.when(it == ITERS - 1)
         def _():
-            out[...] = nn(inverse[...], image, HIGH).T
+            out[...] = nn(inverse[...], image, HIGH)
 
         mirror_done(1, t1, r1, t2, r2, xs, xr)
         band_done(1, wq, rq)
@@ -704,22 +785,25 @@
             to = (z + d) % (2 * COLS)
             z_copy(to, z, to).wait_send()
         back_copy(k).wait_send()
-        gather_z_done(it)
+        pl.when(it > 0)(lambda: gather_z_done(it))
 
     loop(0, ITERS, sweep)
     for d in range(1, COLS):
         to = (c + d) % COLS
         line_band(to, c, to).wait_send()
+        hole_band_copy(to, c, to).wait_send()
 
     @pl.when(zh == 1)
     def _():
         line_far().wait_send()
+        hole_far_copy().wait_send()
 
     @pl.when(zh == 0)
     def _():
         def line_sent(i):
             to = (p + i) % PLANE
             line_plane(to, p, to).wait_send()
+            hole_plane_copy(to, p, to).wait_send()
 
         loop(1, PLANE, line_sent)
 
@@ -757,7 +841,7 @@
     return pl.pallas_call(
         kernel,
         name="subspace",
-        out_shape=jax.ShapeDtypeStruct((BLK, K), F32),
+        out_shape=jax.ShapeDtypeStruct((K, BLK), F32),
         in_specs=[
             pl.BlockSpec(memory_space=pltpu.SMEM),
             pl.BlockSpec(memory_space=pl.ANY),
@@ -793,6 +877,9 @@
             pltpu.VMEM((CHIPS, *line), F32),
             pltpu.VMEM(line, F32),
             pltpu.VMEM(line, F32),
+            pltpu.VMEM((3 * K, start_codes.shape[0]), BF16),
+            pltpu.VMEM((COLS, *line), jnp.int32),
+            pltpu.VMEM((PLANE, *line), jnp.int32),
             pltpu.VMEM((COLS, *line), F32),
             pltpu.VMEM((COLS, *line), F32),
             pltpu.VMEM(block, F32),
@@ -816,6 +903,12 @@
             dma((ITERS, BANDS)),
             dma((ITERS, COLS)),
             dma((ITERS, COLS)),
+            dma((COLS,)),
+            dma((COLS,)),
+            dma((1,)),
+            dma((1,)),
+            dma((PLANE,)),
+            dma((PLANE,)),
             dma((COLS,)),
             dma((COLS,)),
             dma((1,)),
@@ -847,8 +940,8 @@
         block_values.reshape(SLOTS, BLK, BLK),
         near_values,
         hole_ids.reshape(1, BLK),
-        start_codes,
-    )
+        start_codes.T,
+    ).T
 
 
 def solution(mesh):

time: 176 us -> 159 us (0.903)
  Pallas kernels: 171 us -> 156 us
    pallas_call x1, Pallas kernels: 171 us -> 156 us  [shards(): pl.pallas_call(kernel, name='subspace', out_shape=jax.ShapeDtypeStruct((K...]
where the time goes in v3:
time: 159 us
  Pallas kernels  156 us (98%)
  local copies, waits for them, and re-layouts  2.14 us (1%)
    pallas_call x1, Pallas kernels, shards(): pl.pallas_call(kernel, name='subspace', out_shape=jax.ShapeDtypeStruct((K...  156 us

profile of v3, /device:TPU:1, one launch (start us, length us, event | category | flops | bytes accessed | tf_op | source)
XLA Modules:
  0.0 158.9 jit_solution(12907052972060969616)
XLA Ops:
  0.0 0.7 broadcast_maximum_fusion
  0.7 0.2 select_reduce_fusion
  0.9 0.7 concatenate.3.idx
  1.6 155.9 %subspace.1 = f32[64,256]{1,0:T(8,128)} custom-call(s32[384]{0:T(512)} %concatenate.3.idx, bf16[64,256,256]{2,1,0:T(8,128)(2,1)} %bitcast.23, bf16[256,1024]{1,0:T(8,128)(2,1)} %near_hbm.1, s32[1,256]{1,0:T(1,128)} %bitcast.26, f32[64,200]{1,0:T(8,128)} %bitcast.25), custom_call_target="tpu_custom_call" | custom-call | tf_op jit(solution)/shard_map/subspace/pallas_call | solution.py:841
  157.4 1.5 copy.8

commit v4 on v3

--- a/solution.py
+++ b/solution.py
@@ -641,6 +641,26 @@
 
             loop(1, PLANE, arrived)
 
+    def lines_done():
+        for d in range(1, COLS):
+            to = (c + d) % COLS
+            line_band(to, c, to).wait_send()
+            hole_band_copy(to, c, to).wait_send()
+
+        @pl.when(zh == 1)
+        def _():
+            line_far().wait_send()
+            hole_far_copy().wait_send()
+
+        @pl.when(zh == 0)
+        def _():
+            def line_sent(i):
+                to = (p + i) % PLANE
+                line_plane(to, p, to).wait_send()
+                hole_plane_copy(to, p, to).wait_send()
+
+            loop(1, PLANE, line_sent)
+
     def sweep(it):
         @pl.when(it > 0)
         def _():
@@ -662,12 +682,13 @@
         loop(0, SLOTS // GROUP, backward)
         mirror_core(1, chain_c, t1, r1)
 
+        mirror_plane(1, chain_c, t1, r1, t2, r2)
+
         own = jnp.zeros((K, BLK), F32)
         for q in range(COLS):
             own = own + nt(band[q], near[:, q * BLK : (q + 1) * BLK])
         acc[...] = own
 
-        mirror_plane(1, chain_c, t1, r1, t2, r2)
 
         pass_own(it)
         pl.when(it == 0)(lines_wait)
@@ -694,6 +715,7 @@
 
         band_send(1, wq, rq)
         gather_done(it)
+        pl.when(it == 0)(lines_done)
         band_sum(1, acc, wq, rq)
         mirror_sum(1, acc, t1, r1, t2, r2, xs, xr)
 
@@ -704,6 +726,7 @@
         def _():
             band_raw[it + 1, c] = image
             gather_far(it + 1)
+            gather_band(it + 1)
 
         def when_more(stage):
             pl.when(more)(lambda: stage(it + 1))
@@ -745,8 +768,18 @@
         for d in range(1, 2 * COLS):
             to = (z + d) % (2 * COLS)
             z_copy(to, z, to).start()
-        when_more(gather_band)
         when_more(gather_first)
+
+        mirror_done(1, t1, r1, t2, r2, xs, xr)
+        band_done(1, wq, rq)
+        pl.when(it > 0)(lambda: gather_z_done(it))
+        core.wait_send()
+
+        def plane_done(i):
+            to = (p + i) % PLANE
+            plane_copy(to, p, to).wait_send()
+
+        loop(1, PLANE, plane_done)
         for d in range(1, 2 * COLS):
             at = (z + d) % (2 * COLS)
             z_copy(at, at, at).wait_recv()
@@ -761,6 +794,9 @@
 
         back_copy(k).start()
         when_more(gather_second)
+        for d in range(1, 2 * COLS):
+            to = (z + d) % (2 * COLS)
+            z_copy(to, z, to).wait_send()
         back_copy(1 - k).wait_recv()
         low = gram_back[it, 0]
         high = gram_back[it, 1]
@@ -772,40 +808,9 @@
         def _():
             out[...] = nn(inverse[...], image, HIGH)
 
-        mirror_done(1, t1, r1, t2, r2, xs, xr)
-        band_done(1, wq, rq)
-        core.wait_send()
-
-        def plane_done(i):
-            to = (p + i) % PLANE
-            plane_copy(to, p, to).wait_send()
-
-        loop(1, PLANE, plane_done)
-        for d in range(1, 2 * COLS):
-            to = (z + d) % (2 * COLS)
-            z_copy(to, z, to).wait_send()
         back_copy(k).wait_send()
-        pl.when(it > 0)(lambda: gather_z_done(it))
 
     loop(0, ITERS, sweep)
-    for d in range(1, COLS):
-        to = (c + d) % COLS
-        line_band(to, c, to).wait_send()
-        hole_band_copy(to, c, to).wait_send()
-
-    @pl.when(zh == 1)
-    def _():
-        line_far().wait_send()
-        hole_far_copy().wait_send()
-
-    @pl.when(zh == 0)
-    def _():
-        def line_sent(i):
-            to = (p + i) % PLANE
-            line_plane(to, p, to).wait_send()
-            hole_plane_copy(to, p, to).wait_send()
-
-        loop(1, PLANE, line_sent)
 
 
 def shards(block_rows, block_cols, block_values, near_values, hole_ids, start_codes):

time: 159 us -> 155 us (0.975)
  Pallas kernels: 156 us -> 152 us
    pallas_call x1, Pallas kernels: 156 us -> 152 us  [shards(): pl.pallas_call(kernel, name='subspace', out_shape=jax.ShapeDtypeStruct((K...]
where the time goes in v4:
time: 155 us; the launch traced here: 156 us
  Pallas kernels  152 us (98%)
  local copies, waits for them, and re-layouts  2.14 us (1%)
    pallas_call x1, Pallas kernels, shards(): pl.pallas_call(kernel, name='subspace', out_shape=jax.ShapeDtypeStruct((K...  152 us

profile of v4, /device:TPU:1, one launch (start us, length us, event | category | flops | bytes accessed | tf_op | source)
XLA Modules:
  0.0 155.6 jit_solution(300068435467366866)
XLA Ops:
  0.0 0.7 broadcast_maximum_fusion
  0.7 0.2 select_reduce_fusion
  0.9 0.7 concatenate.3.idx
  1.6 152.5 %subspace.1 = f32[64,256]{1,0:T(8,128)} custom-call(s32[384]{0:T(512)} %concatenate.3.idx, bf16[64,256,256]{2,1,0:T(8,128)(2,1)} %bitcast.23, bf16[256,1024]{1,0:T(8,128)(2,1)} %near_hbm.1, s32[1,256]{1,0:T(1,128)} %bitcast.26, f32[64,200]{1,0:T(8,128)} %bitcast.25), custom_call_target="tpu_custom_call" | custom-call | tf_op jit(solution)/shard_map/subspace/pallas_call | solution.py:846
  154.1 1.5 copy.8
